TPU v7x, 512 devices: a whole 4x4x16 slice. The times are simulated.
512 devices in a mesh: dp: 16 (over z), expert: 32 (over y, x, core).
Axes of the slice: x: 4, y: 4, z: 16, core: 2. Of those that a mesh axis runs over, the one named last changes fastest.
Arguments:
- out_grad: bfloat16 [131072, 1440], P(('dp', 'expert')), may hold values from -6 to 6
- gates: float32 [131072], P(('dp', 'expert')), may hold values from 0.05 to 0.6
- expert_ids: int32 [131072], P(('dp', 'expert')), may hold values from 0 to 31, as said below
- saved_gate: bfloat16 [163840, 1440], P(('dp', 'expert')), may hold values from -6 to 6
- saved_up: bfloat16 [163840, 1440], P(('dp', 'expert')), may hold values from -6 to 6
- w_gate: bfloat16 [32, 1440, 1440], P('expert', 'dp'), may hold values from -0.15625 to 0.15625
- w_up: bfloat16 [32, 1440, 1440], P('expert', 'dp'), may hold values from -0.15625 to 0.15625
- w_down: bfloat16 [32, 1440, 1440], P('expert', 'dp'), may hold values from -0.15625 to 0.15625
Outputs:
- d_tokens: bfloat16 [131072, 1440], P(('dp', 'expert'))
- grad_down: float32 [32, 1440, 1440], P('expert', 'dp')
Inputs may be any that keep to these rules, and one draw needn't show every extreme that they name: `expert_ids`: among the tokens of one device, no expert is named by more than 10 tokens; in every draw one expert is named by exactly 10 tokens of every device.
All inputs are finite; a program needn't handle non-finite values.
Results may differ from a plain program's by a relative error of at most 0.019.
Values may be sent and summed in bfloat16 or wider, within the bound.
No kernel may reach another device: no remote copies, remote signals or barrier semaphores. Data moves between devices by JAX's collectives and lax.ppermute only.
A program may use at most 128 MiB of HBM per device.

v0:
```python
import jax
import jax.numpy as jnp
from jax import lax
from jax.sharding import PartitionSpec as P


def contract_last(left, right):
    return lax.dot_general(
        left, right, (((1,), (1,)), ((), ())), preferred_element_type=jnp.float32
    )


def per_device(out_grad, gates, expert_ids, saved_gate, saved_up, w_gate, w_up, w_down):
    n_exp = lax.axis_size("expert")
    slots = saved_gate.shape[0]
    width_d = out_grad.shape[1]
    capacity = slots // n_exp
    onehot = (expert_ids[:, None] == jnp.arange(n_exp, dtype=jnp.int32)[None, :]).astype(jnp.int32)
    earlier = jnp.cumsum(onehot, axis=0) - onehot
    rank = jnp.sum(earlier * onehot, axis=1)
    target = expert_ids * capacity + rank
    placing = (target[:, None] == jnp.arange(slots, dtype=jnp.int32)[None, :]).astype(jnp.bfloat16)
    scaled = (gates[:, None] * out_grad.astype(jnp.float32)).astype(jnp.bfloat16)
    outgoing = lax.dot_general(
        placing, scaled, (((0,), (0,)), ((), ())), preferred_element_type=jnp.float32
    )
    outgoing = outgoing.astype(jnp.bfloat16).reshape(n_exp, capacity, width_d)
    arrived = lax.all_to_all(outgoing, "expert", split_axis=0, concat_axis=0, tiled=True).reshape(
        slots, width_d
    )
    down_shard = w_down[0]
    gate_shard = w_gate[0]
    up_shard = w_up[0]
    dh = contract_last(arrived, lax.all_gather(down_shard, "dp", axis=0, tiled=True))
    gate_pre = saved_gate.astype(jnp.float32)
    up_pre = saved_up.astype(jnp.float32)
    sigma = jax.nn.sigmoid(gate_pre)
    hidden = (gate_pre * sigma * up_pre).astype(jnp.bfloat16)
    d_up = (dh * gate_pre * sigma).astype(jnp.bfloat16)
    d_gate = (dh * up_pre * sigma * (1.0 + gate_pre * (1.0 - sigma))).astype(jnp.bfloat16)
    pieces = lax.all_gather((gate_shard, up_shard), "dp", axis=0, tiled=True)
    d_slots = contract_last(d_gate, pieces[0]) + contract_last(d_up, pieces[1])
    returning = d_slots.astype(jnp.bfloat16).reshape(n_exp, capacity, width_d)
    came_back = lax.all_to_all(
        returning, "expert", split_axis=0, concat_axis=0, tiled=True
    ).reshape(slots, width_d)
    d_tokens = jnp.dot(placing, came_back, preferred_element_type=jnp.float32).astype(jnp.bfloat16)
    grad_local = lax.psum_scatter(
        lax.dot_general(
            hidden, arrived, (((0,), (0,)), ((), ())), preferred_element_type=jnp.float32
        ).astype(jnp.bfloat16),
        "dp",
        scatter_dimension=0,
        tiled=True,
    ).astype(jnp.float32)
    return (d_tokens, grad_local[None])


def solution(mesh):
    in_specs = (
        P(("dp", "expert"), None),
        P(("dp", "expert")),
        P(("dp", "expert")),
        P(("dp", "expert"), None),
        P(("dp", "expert"), None),
        P("expert", "dp", None),
        P("expert", "dp", None),
        P("expert", "dp", None),
    )
    out_specs = (P(("dp", "expert"), None), P("expert", "dp", None))
    return jax.shard_map(
        per_device, mesh=mesh, in_specs=in_specs, out_specs=out_specs, check_vma=False
    )
```

profile of v0, /device:TPU:38, one launch (start us, length us, event | category | flops | bytes accessed | tf_op | source)
XLA Modules:
  0.0 440.7 jit_solution(7521835398061162927)
XLA Ops:
  7.2 0.0 copy-start.1
  7.2 0.0 copy-start.2
  7.2 0.0 all-gather.7.cloned.1.call-start
  7.2 2.2 copy.19
  9.5 0.0 copy-start
  9.5 0.0 copy-start.3
  9.5 0.0 all-gather.7.cloned.1.call-update
  9.5 0.0 all-gather.11.cloned.1.call-start
  9.5 2.2 copy.21
  11.8 0.0 all-gather.11.cloned.1.call-update
  11.8 0.0 all-gather.9.cloned.1.call-start
  11.9 0.0 copy-done.1
  11.9 1.2 copy.20
  13.1 0.0 all-gather.9.cloned.1.call-update
  13.1 0.0 copy-done.2
  13.2 0.6 reduce-window.6
  13.8 0.2 slice_reduce_fusion
  14.0 0.1 fusion.40
  14.1 0.0 copy-done
  14.1 0.0 copy-done.3
  14.1 0.6 convolution_convert_fusion.1
  14.8 0.4 reshape.35
  15.2 28.0 %all_to_all.10 = bf16[32,10,1440]{2,1,0:T(8,128)(2,1)S(1)} all-to-all(bf16[32,10,1440]{2,1,0:T(8,128)(2,1)S(1)} %reshape.35), channel_id=1, replica_groups=mesh['dp'=16,'expert'=32] {'expert'}, dimensions={0} | all-to-all | bytes 1843200 | tf_op jit(solution)/shard_map/all_to_all | solution.py:28
  43.2 0.6 reshape.36
  43.8 6.3 %convolution_convert_fusion = bf16[1440,1440]{1,0:T(8,128)(2,1)} fusion(bf16[320,1440]{1,0:T(8,128)(2,1)S(1)} %reshape.36, bf16[320,1440]{1,0:T(8,128)(2,1)} %param.12, bf16[320,1440]{1,0:T(8,128)(2,1)} %param.11), kind=kOutput, calls=%fused_computation | convolution fusion | flops 1332864000 | bytes 6912000 | tf_op jit(solution)/shard_map/dot_general | solution.py:49
  50.1 0.0 copy-start.4
  50.1 72.7 %all-gather.7.cloned.1.call-done = bf16[1,1440,1440]{2,0,1:T(2,128)(2,1)} async-done(((bf16[1,90,1440]{2,0,1:T(2,128)(2,1)}), bf16[1,1440,1440]{2,0,1:T(2,128)(2,1)}) %all-gather.7.cloned.1.call-update) | async-done | bytes 4147216 | tf_op jit(solution)/shard_map/all_gather | solution.py:34
  122.8 6.5 %fusion.7 = f32[320,1440]{1,0:T(8,128)} fusion(bf16[320,1440]{1,0:T(8,128)(2,1)S(1)} %reshape.36, bf16[1,1440,1440]{2,0,1:T(2,128)(2,1)} %all-gather.7.cloned.1.call-done), kind=kOutput, calls=%fused_computation.7 | convolution fusion | flops 1327104000 | bytes 6912000 | tf_op jit(solution)/shard_map/dot_general | solution.py:8
  129.3 0.0 copy-start.5
  129.3 104.6 %all-gather.11.cloned.1.call-done = bf16[1,1440,1440]{2,0,1:T(2,128)(2,1)} async-done(((bf16[1,90,1440]{2,0,1:T(2,128)(2,1)}), bf16[1,1440,1440]{2,0,1:T(2,128)(2,1)}) %all-gather.11.cloned.1.call-update) | async-done | bytes 4147216 | tf_op jit(solution)/shard_map/all_gather | solution.py:41
  233.9 0.0 copy-done.4
  233.9 7.2 %fusion.1 = f32[320,1440]{1,0:T(8,128)} fusion(bf16[1,1440,1440]{2,0,1:T(2,128)(2,1)} %all-gather.11.cloned.1.call-done, f32[320,1440]{1,0:T(8,128)} %fusion.7, bf16[320,1440]{1,0:T(8,128)(2,1)S(1)} %copy-done.4), kind=kOutput, calls=%fused_computation.1 | convolution fusion | flops 1330329600 | bytes 8755200 | tf_op jit(solution)/shard_map/dot_general | solution.py:8
  241.2 103.3 %all-gather.9.cloned.1.call-done = bf16[1,1440,1440]{2,0,1:T(2,128)(2,1)} async-done(((bf16[1,90,1440]{2,0,1:T(2,128)(2,1)}), bf16[1,1440,1440]{2,0,1:T(2,128)(2,1)}) %all-gather.9.cloned.1.call-update) | async-done | bytes 4147216 | tf_op jit(solution)/shard_map/all_gather | solution.py:41
  344.5 0.0 copy-done.5
  344.5 6.8 %fusion.13 = bf16[320,1440]{1,0:T(8,128)(2,1)S(1)} fusion(f32[320,1440]{1,0:T(8,128)} %fusion.1, bf16[1,1440,1440]{2,0,1:T(2,128)(2,1)} %all-gather.9.cloned.1.call-done, f32[320,1440]{1,0:T(8,128)} %fusion.7, bf16[320,1440]{1,0:T(8,128)(2,1)S(1)} %copy-done.5, bf16[320,1440]{1,0:T(8,128)(2,1)S(1)} %copy-done.4), kind=kOutput, calls=%fused_computation.16 | convolution fusion | flops 1333555200 | bytes 10598400 | tf_op jit(solution)/shard_map/dot_general | solution.py:8
  351.3 1.4 reshape.37
  352.7 7.6 %all-to-all-start.1 = ((bf16[32,10,1440]{2,1,0:T(8,128)(2,1)}), bf16[32,10,1440]{2,1,0:T(8,128)(2,1)S(1)}, u32[]{:S(2)}, u32[]{:S(2)}) async-start(bf16[32,10,1440]{2,1,0:T(8,128)(2,1)} %reshape.37), calls=%async_computation.1 | async-start | bytes 3145728 | tf_op jit(solution)/shard_map/all_to_all | solution.py:44
  360.3 59.6 %fusion = bf16[96,1440]{1,0:T(8,128)(2,1)S(1)} fusion(bf16[1440,1440]{1,0:T(8,128)(2,1)} %convolution_convert_fusion), kind=kCustom, calls=%all-reduce-scatter | all-reduce-scatter fusion | flops 2211841 | bytes 4425728
  419.9 0.1 slice.9
  420.0 2.1 collective-permute-start
  422.1 1.3 dynamic-slice.4
  424.0 5.8 %collective-permute-done = bf16[90,1440]{1,0:T(8,128)(2,1)S(1)} collective-permute-done((bf16[90,1440]{1,0:T(8,128)(2,1)S(1)}, bf16[90,1440]{1,0:T(8,128)(2,1)S(1)}, u32[]{:S(2)}, u32[]{:S(2)}) %collective-permute-start) | collective-permute-done | bytes 259232
  429.8 0.7 concatenate
  430.5 0.1 fusion.34
  430.6 1.4 copy.22
  432.0 0.0 all-to-all-done.1
  432.0 0.6 reshape.38
  432.6 1.5 convolution_convert_fusion.2
  (4 shorter events, 0.1 us)
Async XLA Ops:
  7.2 4.7 %copy-start.1 = (bf16[1,90,1440]{2,1,0:T(8,128)(2,1)S(1)}, bf16[1,90,1440]{2,1,0:T(8,128)(2,1)}, u32[]{:S(2)}) copy-start(bf16[1,90,1440]{2,1,0:T(8,128)(2,1)} %param.13) | copy-start | bytes 777604
  7.2 6.0 %copy-start.2 = (s32[256]{0:T(256)S(1)}, s32[256]{0:T(256)}, u32[]{:S(2)}) copy-start(s32[256]{0:T(256)} %param.10) | copy-start | bytes 3076
  7.2 115.6 %all-gather.7.cloned.1.call-start = ((), (), s32[]{:S(2)}) async-start(), calls=%async_computation.2 | async-start | bytes 9400320 | tf_op jit(solution)/shard_map/all_gather | solution.py:34
  9.5 4.6 %copy-start = (bf16[256,1440]{0,1:T(8,128)(2,1)S(1)}, bf16[256,1440]{0,1:T(8,128)(2,1)}, u32[]{:S(2)}) copy-start(bf16[256,1440]{0,1:T(8,128)(2,1)} %param.8) | copy-start | bytes 2211844
  9.5 4.7 %copy-start.3 = (f32[256]{0:T(256)S(1)}, f32[256]{0:T(256)}, u32[]{:S(2)}) copy-start(f32[256]{0:T(256)} %param.9) | copy-start | bytes 3076
  9.5 224.4 %all-gather.11.cloned.1.call-start = ((), (), s32[]{:S(2)}) async-start(), calls=%async_computation.4 | async-start | bytes 9400320 | tf_op jit(solution)/shard_map/all_gather | solution.py:41
  11.8 332.7 %all-gather.9.cloned.1.call-start = ((), (), s32[]{:S(2)}) async-start(), calls=%async_computation.3 | async-start | bytes 9400320 | tf_op jit(solution)/shard_map/all_gather | solution.py:41
  50.1 183.9 %copy-start.4 = (bf16[320,1440]{1,0:T(8,128)(2,1)S(1)}, bf16[320,1440]{1,0:T(8,128)(2,1)}, u32[]{:S(2)}) copy-start(bf16[320,1440]{1,0:T(8,128)(2,1)} %param.11) | copy-start | bytes 2764804
  129.3 215.2 %copy-start.5 = (bf16[320,1440]{1,0:T(8,128)(2,1)S(1)}, bf16[320,1440]{1,0:T(8,128)(2,1)}, u32[]{:S(2)}) copy-start(bf16[320,1440]{1,0:T(8,128)(2,1)} %param.12) | copy-start | bytes 2764804
  352.7 79.3 %all-to-all-start.1 = ((bf16[32,10,1440]{2,1,0:T(8,128)(2,1)}), bf16[32,10,1440]{2,1,0:T(8,128)(2,1)S(1)}, u32[]{:S(2)}, u32[]{:S(2)}) async-start(bf16[32,10,1440]{2,1,0:T(8,128)(2,1)} %reshape.37), calls=%async_computation.1 | async-start | bytes 3145728 | tf_op jit(solution)/shard_map/all_to_all | solution.py:44
  420.0 9.8 %collective-permute-start = (bf16[90,1440]{1,0:T(8,128)(2,1)S(1)}, bf16[90,1440]{1,0:T(8,128)(2,1)S(1)}, u32[]{:S(2)}, u32[]{:S(2)}) collective-permute-start(bf16[90,1440]{1,0:T(8,128)(2,1)S(1)} %slice.9), channel_id=1, source_target_pairs={{0,32},{32,64},{64,96},{96,128},{128,160},{160,192},{192,224},{224... | collective-permute-start | bytes 777608
Sparse Core Ops, SparseCore 0:
  10.7 112.0 all-gather.6
  125.4 108.4 all-gather.10
  236.0 108.4 all-gather.8
where the time goes:
time: 441 us
  waiting for transfers between devices  287 us (65%)
  blocking collectives  87.6 us (20%)
  matrix products  29 us (7%)
  between operations  14.6 us (3%)
  local copies, waits for them, and re-layouts  12.4 us (3%)
  starting transfers between devices  9.77 us (2%)
    all_gather x2, waiting for transfers between devices, per_device(): pieces = lax.all_gather((gate_shard, up_shard), 'dp', axis=0, tiled=True)  208 us
    all_gather x1, waiting for transfers between devices, per_device(): lax.all_gather(down_shard, 'dp', axis=0, tiled=True)  72.7 us
    unnamed x1, blocking collectives  59.6 us
    all_to_all x1, blocking collectives, per_device(): lax.all_to_all(outgoing, 'expert', split_axis=0, concat_axis=0, tiled=True)  28 us
    dot_general x3, matrix products, contract_last(): lax.dot_general(left, right, (((1,), (1,)), ((), ())), preferred_element_...  20.5 us
    unnamed x19, local copies, waits for them, and re-layouts  9.17 us
  transfers between devices with their start and end apart: 5, of which 4 were waited for; matrix products, arithmetic and copies ran while one was open for 20% of the time, Pallas kernels for 0%

commit v1 on v0

v1 whole, which is shorter than its diff:
```python
import jax
import jax.numpy as jnp
from jax import lax
from jax.experimental import pallas as pl
from jax.experimental.pallas import tpu as pltpu
from jax.sharding import PartitionSpec as P

HALF = 48
RING = 80


def contract_last(left, right):
    return lax.dot_general(
        left, right, (((1,), (1,)), ((), ())), preferred_element_type=jnp.float32
    )


def contract_first(left, right):
    return lax.dot_general(
        left, right, (((0,), (0,)), ((), ())), preferred_element_type=jnp.float32
    )


def shift(block, by, n):
    return lax.ppermute(block, "dp", [(i, (i + by) % n) for i in range(n)])


def stacked_matmul_kernel(*refs):
    left = refs[0]
    blocks = refs[1:-3]
    out, stack, sems = refs[-3:]
    copies, ends, at = [], [], 0
    for i, block in enumerate(blocks):
        copies.append(
            pltpu.make_async_copy(block, stack.at[pl.ds(at, block.shape[0])], sems.at[i])
        )
        at += block.shape[0]
        ends.append(at)
    for copy in copies:
        copy.start()
    done = 0
    for copy, end in zip(copies, ends):
        copy.wait()
        if (end - done >= 256 and end % 128 == 0) or end == at:
            rows = pl.ds(done, end - done)
            out[:, rows] = contract_last(left[...], stack[rows, :]).astype(out.dtype)
            done = end


def stacked_matmul(left, blocks):
    rows, depth = left.shape
    count = sum(block.shape[0] for block in blocks)
    return pl.pallas_call(
        stacked_matmul_kernel,
        out_shape=jax.ShapeDtypeStruct((rows, count), jnp.bfloat16),
        in_specs=[pl.BlockSpec(memory_space=pltpu.VMEM)]
        + [pl.BlockSpec(memory_space=pl.ANY)] * len(blocks),
        out_specs=pl.BlockSpec(memory_space=pltpu.VMEM),
        scratch_shapes=[
            pltpu.VMEM((count, depth), jnp.bfloat16),
            pltpu.SemaphoreType.DMA((len(blocks),)),
        ],
        compiler_params=pltpu.CompilerParams(vmem_limit_bytes=56 * 2**20),
        cost_estimate=pl.CostEstimate(
            flops=2 * rows * depth * count,
            bytes_accessed=2 * depth * (count + rows),
            transcendentals=0,
        ),
    )(left, *blocks)


def per_device(out_grad, gates, expert_ids, saved_gate, saved_up, w_gate, w_up, w_down):
    n_exp = lax.axis_size("expert")
    n_dp = lax.axis_size("dp")
    me = lax.axis_index("dp")
    slots, width_f = saved_gate.shape
    width_d = out_grad.shape[1]
    capacity = slots // n_exp
    rows = w_down.shape[1]
    part = rows // 2
    bf16 = jnp.bfloat16

    pair = jnp.concatenate([w_gate[0], w_up[0]], axis=1)
    down = jnp.concatenate([w_down[0, :part], w_down[0, part:]], axis=1)
    down = jnp.concatenate([down, pair[RING:]])
    deep = -(-down.shape[0] // 8) * 8
    gathered = lax.all_gather(
        jnp.pad(down, ((0, deep - down.shape[0]), (0, 0))), "dp", axis=0, tiled=False
    )
    down = gathered.reshape(n_dp * deep, 2 * width_d)
    rest = gathered[:, part : part + rows - RING].reshape(n_dp * (rows - RING), 2 * width_d)
    own = pair[:RING]

    right, left = shift(own, 1, n_dp), shift(own, -1, n_dp)
    steps = [(right, left)]

    onehot = (expert_ids[:, None] == jnp.arange(n_exp, dtype=jnp.int32)[None, :]).astype(jnp.int32)
    earlier = jnp.cumsum(onehot, axis=0) - onehot
    rank = jnp.sum(earlier * onehot, axis=1)
    target = expert_ids * capacity + rank
    placing = (target[:, None] == jnp.arange(slots, dtype=jnp.int32)[None, :]).astype(bf16)
    scaled = (gates[:, None] * out_grad.astype(jnp.float32)).astype(bf16)
    outgoing = contract_first(placing, scaled).astype(bf16).reshape(n_exp, capacity, width_d)

    unit = jnp.arange(width_f, dtype=jnp.int32)
    side = unit // part % 2

    def spreading(stride):
        at = unit // rows * stride + unit % part
        column = jnp.arange(n_dp * stride, dtype=jnp.int32)[None, :]
        return [((at[:, None] == column) & (side[:, None] == h)).astype(bf16) for h in (0, 1)]

    def spread_out(a, spread):
        return jnp.concatenate(
            [jnp.dot(a, s, preferred_element_type=jnp.float32).astype(bf16) for s in spread]
        )

    def gather_in(a, spread):
        return (contract_last(a[:slots], spread[0]) + contract_last(a[slots:], spread[1])).astype(bf16)

    gate_f = saved_gate.astype(jnp.float32)
    hidden = (gate_f * jax.nn.sigmoid(gate_f) * saved_up.astype(jnp.float32)).astype(bf16)
    right, left, outgoing, hidden = lax.optimization_barrier((right, left, outgoing, hidden))

    right, left = shift(right, 1, n_dp), shift(left, -1, n_dp)
    arrived = lax.all_to_all(outgoing, "expert", split_axis=0, concat_axis=0, tiled=True)
    hidden = spread_out(hidden, spreading(HALF))
    right, left, hidden = lax.optimization_barrier((right, left, hidden))
    steps.append((right, left))

    right, left = shift(right, 1, n_dp), shift(left, -1, n_dp)
    spread = spreading(deep)
    gate_pre = spread_out(saved_gate, spread)
    up_pre = spread_out(saved_up, spread)
    right, left, arrived, gate_pre, up_pre = lax.optimization_barrier(
        (right, left, arrived, gate_pre, up_pre)
    )
    steps.append((right, left))

    right, left = shift(right, 1, n_dp), shift(left, -1, n_dp)
    arrived = arrived.reshape(slots, width_d)
    none = jnp.zeros_like(arrived)
    twice = jnp.concatenate(
        [jnp.concatenate([arrived, none], axis=1), jnp.concatenate([none, arrived], axis=1)]
    )
    right, left, twice = lax.optimization_barrier((right, left, twice))
    steps.append((right, left))

    partial = contract_first(hidden, twice).astype(bf16)
    grad = lax.psum_scatter(partial, "dp", scatter_dimension=0, tiled=True)[:part]
    grad = jnp.concatenate([grad[:, :width_d], grad[:, width_d:]]).astype(jnp.float32)
    right, left = shift(right, 1, n_dp), shift(left, -1, n_dp)
    right, left, down, rest = lax.optimization_barrier((right, left, down, rest))
    steps.append((right, left))

    right, left = shift(right, 1, n_dp), shift(left, -1, n_dp)
    dh = contract_last(twice, down)
    gate_pre = gate_pre.astype(jnp.float32)
    up_pre = up_pre.astype(jnp.float32)
    sigma = jax.nn.sigmoid(gate_pre)
    d_up = (dh * gate_pre * sigma).astype(bf16)
    d_gate = (dh * up_pre * sigma * (1.0 + gate_pre * (1.0 - sigma))).astype(bf16)
    both = jnp.concatenate([gather_in(d_gate, spread), gather_in(d_up, spread)], axis=1)
    right, left, both = lax.optimization_barrier((right, left, both))
    steps.append((right, left))

    def exchange(back):
        back = back.reshape(n_exp, capacity, -1)
        back = lax.all_to_all(back, "expert", split_axis=0, concat_axis=0, tiled=True)
        return back.reshape(slots, -1)

    def result(back, places):
        mine = jnp.dot(placing, back, preferred_element_type=jnp.float32).astype(bf16)
        order = jnp.concatenate(places)[:, None] == jnp.arange(width_d, dtype=jnp.int32)[None, :]
        return jnp.dot(mine, order.astype(bf16), preferred_element_type=jnp.float32)

    def place(offset):
        return (me + offset + n_dp) % n_dp * rows + jnp.arange(RING, dtype=jnp.int32)

    right, left = shift(right, 1, n_dp), shift(left, -1, n_dp)
    extra = jnp.arange(n_dp * (rows - RING), dtype=jnp.int32)
    blocks = [rest, own]
    places = [extra // (rows - RING) * rows + RING + extra % (rows - RING), place(0)]
    for step, pieces in enumerate(steps, 1):
        blocks += pieces
        places += [place(-step), place(step)]
    early = stacked_matmul(both, blocks)
    right, left, early = lax.optimization_barrier((right, left, early))

    cut = RING // 32 * 16 + 16
    ends = [shift(right[:cut], 1, n_dp), shift(left[cut:], -1, n_dp)]
    early = result(exchange(early), places).astype(bf16)
    ends[0], ends[1], early = lax.optimization_barrier((ends[0], ends[1], early))
    late = stacked_matmul(both, [right, left] + ends)
    last = n_dp // 2
    late = result(exchange(late), [place(1 - last), place(last - 1), place(last)])
    d_tokens = (early.astype(jnp.float32) + late).astype(bf16)
    return (d_tokens, grad[None])


def solution(mesh):
    in_specs = (
        P(("dp", "expert"), None),
        P(("dp", "expert")),
        P(("dp", "expert")),
        P(("dp", "expert"), None),
        P(("dp", "expert"), None),
        P("expert", "dp", None),
        P("expert", "dp", None),
        P("expert", "dp", None),
    )
    out_specs = (P(("dp", "expert"), None), P("expert", "dp", None))
    return jax.shard_map(
        per_device, mesh=mesh, in_specs=in_specs, out_specs=out_specs, check_vma=False
    )
```

time: 441 us -> 257 us (0.58)
  the two profiles are of different devices: /device:TPU:38 before, /device:TPU:97 now
where the time goes in v1:
time: 257 us; the launch traced here: 256 us
  waiting for transfers between devices  87.8 us (34%)
  starting transfers between devices  73.3 us (29%)
  matrix products  36.6 us (14%)
  local copies, waits for them, and re-layouts  17.3 us (7%)
  between operations  14.9 us (6%)
  Pallas kernels  13.1 us (5%)
  other arithmetic  12.9 us (5%)
    ppermute x16, waiting for transfers between devices, shift(): return lax.ppermute(block, 'dp', [(i, (i + by) % n) for i in range(n)])  68.4 us
    ppermute x16, starting transfers between devices, shift(): return lax.ppermute(block, 'dp', [(i, (i + by) % n) for i in range(n)])  45 us
    all_to_all x2, waiting for transfers between devices, exchange(): lax.all_to_all(back, 'expert', split_axis=0, concat_axis=0, tiled=True)  18.8 us
    all_to_all x2, starting transfers between devices, exchange(): lax.all_to_all(back, 'expert', split_axis=0, concat_axis=0, tiled=True)  18.8 us
    dot_general x5, matrix products, contract_last(): lax.dot_general(left, right, (((1,), (1,)), ((), ())), preferred_element_...  14.9 us
    pallas_call x2, Pallas kernels, stacked_matmul(): pl.pallas_call(stacked_matmul_kernel, out_shape=jax.ShapeDtypeStruct((row...  13.1 us
    dot_general x6, matrix products, spread_out(): jnp.dot(a, s, preferred_element_type=jnp.float32).astype(bf16)  11.7 us
    all_to_all x1, starting transfers between devices, per_device(): lax.all_to_all(outgoing, 'expert', split_axis=0, concat_axis=0, tiled=True)  9.52 us
  transfers between devices with their start and end apart: 21, of which 15 were waited for; matrix products, arithmetic and copies ran while one was open for 23% of the time, Pallas kernels for 3%

profile of v1, /device:TPU:97, one launch (start us, length us, event | category | flops | bytes accessed | tf_op | source)
XLA Modules:
  0.0 255.9 jit_solution(5035647673285863932)
XLA Ops:
  7.3 1.1 slice_bitcast_fusion.3
  8.4 1.1 fusion.117
  10.5 4.8 %collective-permute-start = (bf16[80,2880]{1,0:T(8,128)(2,1)S(1)}, bf16[80,2880]{1,0:T(8,128)(2,1)}, u32[]{:S(2)}, u32[]{:S(2)}) collective-permute-start(bf16[80,2880]{1,0:T(8,128)(2,1)S(1)} %fusion.114.refs_2_), channel_id=1, source_target_pairs={{0,32},{32,64},{64,96},{96,128},{128,160},{160,192},{192,224},{224... | collective-permute-start | bytes 1382408 | tf_op jit(solution)/shard_map/ppermute | solution.py:25
  15.3 1.9 collective-permute-start.1
  18.8 1.4 reshape.130
  20.4 1.5 fusion.100
  21.9 2.3 fusion.103
  24.2 2.4 fusion.94
  26.6 1.6 fusion.74
  28.2 1.6 collective-permute-done.1.refs_4_
  29.8 2.9 %collective-permute-start.2 = (bf16[80,2880]{1,0:T(8,128)(2,1)}, bf16[80,2880]{1,0:T(8,128)(2,1)}, u32[]{:S(2)}, u32[]{:S(2)}) collective-permute-start(bf16[80,2880]{1,0:T(8,128)(2,1)} %collective-permute-done.refs_3_), channel_id=1, source_target_pairs={{0,32},{32,64},{64,96},{96,128},{128,160},{160,192},{192,224},{224... | collective-permute-start | bytes 1382408 | tf_op jit(solution)/shard_map/ppermute | solution.py:25
  32.7 2.3 collective-permute-start.3
  35.1 9.5 %all-to-all-start = ((bf16[32,10,1440]{2,1,0:T(8,128)(2,1)}), bf16[32,10,1440]{2,1,0:T(8,128)(2,1)S(1)}, u32[]{:S(2)}, u32[]{:S(2)}) async-start(bf16[32,10,1440]{2,1,0:T(8,128)(2,1)} %reshape.130), calls=%async_computation | async-start | bytes 3145728 | tf_op jit(solution)/shard_map/all_to_all | solution.py:126
  44.7 2.6 %fusion.88 = bf16[320,768]{1,0:T(8,128)(2,1)S(1)} fusion(bf16[320,1440]{1,0:T(8,128)(2,1)} %fusion.74, s32[1440]{0:T(1024)S(1)} %fusion.136, pred[1440]{0:T(1024)(128)(4,1)S(1)} %broadcast_compare_fusion.1), kind=kOutput, calls=%fused_computation.79 | convolution fusion | flops 710246400 | bytes 1420320 | tf_op jit(solution)/shard_map/dot_general | solution.py:115
  47.3 1.4 fusion.91
  48.7 1.1 pad_maximum_fusion.3
  49.8 4.3 %collective-permute-done.2.refs_5_ = bf16[80,2880]{1,0:T(8,128)(2,1)} collective-permute-done((bf16[80,2880]{1,0:T(8,128)(2,1)}, bf16[80,2880]{1,0:T(8,128)(2,1)}, u32[]{:S(2)}, u32[]{:S(2)}) %collective-permute-start.2) | collective-permute-done | bytes 460832 | tf_op jit(solution)/shard_map/ppermute | solution.py:25
  54.1 3.8 %collective-permute-done.3.refs_6_ = bf16[80,2880]{1,0:T(8,128)(2,1)} collective-permute-done((bf16[80,2880]{1,0:T(8,128)(2,1)}, bf16[80,2880]{1,0:T(8,128)(2,1)}, u32[]{:S(2)}, u32[]{:S(2)}) %collective-permute-start.3) | collective-permute-done | bytes 460832 | tf_op jit(solution)/shard_map/ppermute | solution.py:25
  57.9 3.7 %collective-permute-start.4 = (bf16[80,2880]{1,0:T(8,128)(2,1)}, bf16[80,2880]{1,0:T(8,128)(2,1)}, u32[]{:S(2)}, u32[]{:S(2)}) collective-permute-start(bf16[80,2880]{1,0:T(8,128)(2,1)} %collective-permute-done.2.refs_5_), channel_id=1, source_target_pairs={{0,32},{32,64},{64,96},{96,128},{128,160},{160,192},{192,224},{224... | collective-permute-start | bytes 1382408 | tf_op jit(solution)/shard_map/ppermute | solution.py:25
  61.6 1.9 collective-permute-start.5
  63.6 1.5 fusion.97
  65.1 1.2 pad_maximum_fusion.1
  66.8 15.0 %collective-permute-done.4.refs_7_ = bf16[80,2880]{1,0:T(8,128)(2,1)} collective-permute-done((bf16[80,2880]{1,0:T(8,128)(2,1)}, bf16[80,2880]{1,0:T(8,128)(2,1)}, u32[]{:S(2)}, u32[]{:S(2)}) %collective-permute-start.4) | collective-permute-done | bytes 460832 | tf_op jit(solution)/shard_map/ppermute | solution.py:25
  81.8 4.5 %collective-permute-done.5.refs_8_ = bf16[80,2880]{1,0:T(8,128)(2,1)} collective-permute-done((bf16[80,2880]{1,0:T(8,128)(2,1)}, bf16[80,2880]{1,0:T(8,128)(2,1)}, u32[]{:S(2)}, u32[]{:S(2)}) %collective-permute-start.5) | collective-permute-done | bytes 460832 | tf_op jit(solution)/shard_map/ppermute | solution.py:25
  86.4 2.8 %collective-permute-start.6 = (bf16[80,2880]{1,0:T(8,128)(2,1)}, bf16[80,2880]{1,0:T(8,128)(2,1)S(1)}, u32[]{:S(2)}, u32[]{:S(2)}) collective-permute-start(bf16[80,2880]{1,0:T(8,128)(2,1)} %collective-permute-done.4.refs_7_), channel_id=1, source_target_pairs={{0,32},{32,64},{64,96},{96,128},{128,160},{160,192},{192,224},{224... | collective-permute-start | bytes 1382408 | tf_op jit(solution)/shard_map/ppermute | solution.py:25
  89.2 2.6 %collective-permute-start.7 = (bf16[80,2880]{1,0:T(8,128)(2,1)}, bf16[80,2880]{1,0:T(8,128)(2,1)}, u32[]{:S(2)}, u32[]{:S(2)}) collective-permute-start(bf16[80,2880]{1,0:T(8,128)(2,1)} %collective-permute-done.5.refs_8_), channel_id=1, source_target_pairs={{0,480},{32,0},{64,32},{96,64},{128,96},{160,128},{192,160},{224,1... | collective-permute-start | bytes 1382408 | tf_op jit(solution)/shard_map/ppermute | solution.py:25
  91.8 1.4 reshape.131
  93.2 2.2 fusion.27
  95.4 14.6 %collective-permute-done.6.refs_9_ = bf16[80,2880]{1,0:T(8,128)(2,1)S(1)} collective-permute-done((bf16[80,2880]{1,0:T(8,128)(2,1)}, bf16[80,2880]{1,0:T(8,128)(2,1)S(1)}, u32[]{:S(2)}, u32[]{:S(2)}) %collective-permute-start.6) | collective-permute-done | bytes 460832 | tf_op jit(solution)/shard_map/ppermute | solution.py:25
  110.0 4.8 %collective-permute-done.7.refs_10_ = bf16[80,2880]{1,0:T(8,128)(2,1)} collective-permute-done((bf16[80,2880]{1,0:T(8,128)(2,1)}, bf16[80,2880]{1,0:T(8,128)(2,1)}, u32[]{:S(2)}, u32[]{:S(2)}) %collective-permute-start.7) | collective-permute-done | bytes 460832 | tf_op jit(solution)/shard_map/ppermute | solution.py:25
  114.8 5.5 %convolution_convert_fusion = bf16[768,2880]{1,0:T(8,128)(2,1)} fusion(bf16[640,768]{1,0:T(8,128)(2,1)S(1)} %copy-done.8, bf16[640,2880]{1,0:T(8,128)(2,1)S(1)} %fusion.27), kind=kOutput, calls=%fused_computation.17 | convolution fusion | flops 2833367040 | bytes 9093120 | tf_op jit(solution)/shard_map/dot_general | solution.py:19
  120.3 3.4 %collective-permute-start.8 = (bf16[80,2880]{1,0:T(8,128)(2,1)S(1)}, bf16[80,2880]{1,0:T(8,128)(2,1)}, u32[]{:S(2)}, u32[]{:S(2)}) collective-permute-start(bf16[80,2880]{1,0:T(8,128)(2,1)S(1)} %collective-permute-done.6.refs_9_), channel_id=1, source_target_pairs={{0,32},{32,64},{64,96},{96,128},{128,160},{160,192},{192,224},{224... | collective-permute-start | bytes 1382408 | tf_op jit(solution)/shard_map/ppermute | solution.py:25
  123.7 1.9 collective-permute-start.9
  125.8 1.7 slice.66
  127.6 1.4 reshape.133.refs_1_
  129.0 1.7 collective-permute-done.8.refs_11_
  130.6 4.4 %collective-permute-done.9.refs_12_ = bf16[80,2880]{1,0:T(8,128)(2,1)} collective-permute-done((bf16[80,2880]{1,0:T(8,128)(2,1)}, bf16[80,2880]{1,0:T(8,128)(2,1)}, u32[]{:S(2)}, u32[]{:S(2)}) %collective-permute-start.9) | collective-permute-done | bytes 460832 | tf_op jit(solution)/shard_map/ppermute | solution.py:25
  135.0 1.9 collective-permute-start.10
  137.0 3.4 %collective-permute-start.11 = (bf16[80,2880]{1,0:T(8,128)(2,1)}, bf16[80,2880]{1,0:T(8,128)(2,1)S(1)}, u32[]{:S(2)}, u32[]{:S(2)}) collective-permute-start(bf16[80,2880]{1,0:T(8,128)(2,1)} %collective-permute-done.9.refs_12_), channel_id=1, source_target_pairs={{0,480},{32,0},{64,32},{96,64},{128,96},{160,128},{192,160},{224,1... | collective-permute-start | bytes 1382408 | tf_op jit(solution)/shard_map/ppermute | solution.py:25
  140.3 8.9 %fusion.145 = f32[640,896]{1,0:T(8,128)S(1)} fusion(bf16[640,2880]{1,0:T(8,128)(2,1)} %copy-done.1, bf16[896,2880]{1,0:T(8,128)(2,1)} %all-gather.3.cloned.1.call-done), kind=kOutput, calls=%fused_computation.174 | convolution fusion | flops 3303014400 | bytes 11141120 | tf_op jit(solution)/shard_map/dot_general | solution.py:13
  149.2 1.1 fusion.63
  150.4 1.5 fusion.7
  151.9 1.5 fusion.5
  153.3 1.5 fusion.38
  154.9 1.5 fusion.35
  156.4 1.8 pad_maximum_fusion.refs_0_
  158.2 2.5 collective-permute-done.11.refs_14_
  160.7 4.0 %collective-permute-start.12 = (bf16[80,2880]{1,0:T(8,128)(2,1)S(1)}, bf16[80,2880]{1,0:T(8,128)(2,1)S(1)}, u32[]{:S(2)}, u32[]{:S(2)}) collective-permute-start(bf16[80,2880]{1,0:T(8,128)(2,1)S(1)} %collective-permute-done.10.refs_13_), channel_id=1, source_target_pairs={{0,32},{32,64},{64,96},{96,128},{128,160},{160,192},{192,224},{224... | collective-permute-start | bytes 1382408 | tf_op jit(solution)/shard_map/ppermute | solution.py:25
  164.7 2.1 collective-permute-start.13
  167.6 8.9 %shard_map.95 = bf16[320,1200]{1,0:T(8,128)(2,1)} custom-call(bf16[320,2880]{1,0:T(8,128)(2,1)} %pad_maximum_fusion.refs_0_, bf16[160,2880]{1,0:T(8,128)(2,1)} %reshape.133.refs_1_, bf16[80,2880]{1,0:T(8,128)(2,1)} %copy-done.2, bf16[80,2880]{1,0:T(8,128)(2,1)} %collective-permute-done.refs_3_, bf16[80,2880]{1,0:T(8,128)(2,1)} %collective-permute-done.1.refs_4_, ...), custom_call_target="tpu_custom_call" | custom-call | flops 2211840000 | bytes 8755200 | tf_op jit(solution)/shard_map/pallas_call | solution.py:53
  176.5 5.5 %collective-permute-done.12.refs_1_ = bf16[80,2880]{1,0:T(8,128)(2,1)S(1)} collective-permute-done((bf16[80,2880]{1,0:T(8,128)(2,1)S(1)}, bf16[80,2880]{1,0:T(8,128)(2,1)S(1)}, u32[]{:S(2)}, u32[]{:S(2)}) %collective-permute-start.12) | collective-permute-done | bytes 460832 | tf_op jit(solution)/shard_map/ppermute | solution.py:25
  182.0 5.6 %collective-permute-done.13.refs_2_ = bf16[80,2880]{1,0:T(8,128)(2,1)S(1)} collective-permute-done((bf16[80,2880]{1,0:T(8,128)(2,1)S(1)}, bf16[80,2880]{1,0:T(8,128)(2,1)S(1)}, u32[]{:S(2)}, u32[]{:S(2)}) %collective-permute-start.13) | collective-permute-done | bytes 460832 | tf_op jit(solution)/shard_map/ppermute | solution.py:25
  187.7 2.4 reshape.134
  190.1 13.3 %all-to-all-start.1 = ((bf16[32,10,1200]{2,1,0:T(8,128)(2,1)}), bf16[32,10,1200]{2,1,0:T(8,128)(2,1)S(1)}, u32[]{:S(2)}, u32[]{:S(2)}) async-start(bf16[32,10,1200]{2,1,0:T(8,128)(2,1)} %reshape.134), calls=%async_computation.1 | async-start | bytes 2621440 | tf_op jit(solution)/shard_map/all_to_all | solution.py:169
  204.8 1.9 collective-permute-start.14
  206.7 3.4 %collective-permute-start.15 = (bf16[32,2880]{1,0:T(8,128)(2,1)S(1)}, bf16[32,2880]{1,0:T(8,128)(2,1)S(1)}, u32[]{:S(2)}, u32[]{:S(2)}) collective-permute-start(bf16[32,2880]{1,0:T(8,128)(2,1)S(1)} %slice.60), channel_id=1, source_target_pairs={{0,480},{32,0},{64,32},{96,64},{128,96},{160,128},{192,160},{224,1... | collective-permute-start | bytes 552968 | tf_op jit(solution)/shard_map/ppermute | solution.py:25
  210.1 1.1 slice_bitcast_fusion.1
  211.2 11.2 %all-to-all-done.1 = bf16[32,10,1200]{2,1,0:T(8,128)(2,1)S(1)} async-done(((bf16[32,10,1200]{2,1,0:T(8,128)(2,1)}), bf16[32,10,1200]{2,1,0:T(8,128)(2,1)S(1)}, u32[]{:S(2)}, u32[]{:S(2)}) %all-to-all-start.1) | async-done | bytes 768032 | tf_op jit(solution)/shard_map/all_to_all | solution.py:169
  223.0 3.2 %fusion.41 = bf16[256,1440]{0,1:T(8,128)(2,1)S(1)} fusion(s32[1200]{0:T(1024)} %concatenate.60, bf16[320,1200]{1,0:T(8,128)(2,1)S(1)} %reshape.135, s32[256]{0:T(256)} %copy-done.19), kind=kOutput, calls=%fused_computation.33 | convolution fusion | flops 1083829760 | bytes 1511104 | tf_op jit(solution)/shard_map/dot_general | solution.py:175
  226.8 4.2 %shard_map.96 = bf16[320,240]{1,0:T(8,128)(2,1)} custom-call(bf16[320,2880]{1,0:T(8,128)(2,1)} %pad_maximum_fusion.refs_0_, bf16[80,2880]{1,0:T(8,128)(2,1)} %copy-done.3, bf16[80,2880]{1,0:T(8,128)(2,1)} %copy-done.10, bf16[48,2880]{1,0:T(8,128)(2,1)} %collective-permute-done.14.refs_3_, bf16[32,2880]{1,0:T(8,128)(2,1)} %copy-done.17), custom_call_target="tpu_custom_call" | custom-call | flops 442368000 | bytes 3225600 | tf_op jit(solution)/shard_map/pallas_call | solution.py:53
  231.1 1.7 reshape.136
  232.8 5.5 %all-to-all-start.2 = ((bf16[32,10,240]{2,1,0:T(8,128)(2,1)}), bf16[32,10,240]{2,1,0:T(8,128)(2,1)S(1)}, u32[]{:S(2)}, u32[]{:S(2)}) async-start(bf16[32,10,240]{2,1,0:T(8,128)(2,1)} %reshape.136), calls=%async_computation.2 | async-start | bytes 524288 | tf_op jit(solution)/shard_map/all_to_all | solution.py:169
  238.3 1.4 copy.12
  239.7 7.6 %all-to-all-done.2 = bf16[32,10,240]{2,1,0:T(8,128)(2,1)S(1)} async-done(((bf16[32,10,240]{2,1,0:T(8,128)(2,1)}), bf16[32,10,240]{2,1,0:T(8,128)(2,1)S(1)}, u32[]{:S(2)}, u32[]{:S(2)}) %all-to-all-start.2) | async-done | bytes 153632 | tf_op jit(solution)/shard_map/all_to_all | solution.py:169
  (90 shorter events, 8.5 us)
Async XLA Ops:
  7.2 3.2 %copy-start.5 = (bf16[1,90,1440]{2,1,0:T(8,128)(2,1)S(1)}, bf16[1,90,1440]{2,1,0:T(8,128)(2,1)}, u32[]{:S(2)}) copy-start(bf16[1,90,1440]{2,1,0:T(8,128)(2,1)} %param.13) | copy-start | bytes 777604
  7.2 3.2 %copy-start.4 = (bf16[1,90,1440]{2,1,0:T(8,128)(2,1)S(1)}, bf16[1,90,1440]{2,1,0:T(8,128)(2,1)}, u32[]{:S(2)}) copy-start(bf16[1,90,1440]{2,1,0:T(8,128)(2,1)} %param.14) | copy-start | bytes 777604
  7.2 10.0 %copy-start.18 = (s32[256]{0:T(256)S(1)}, s32[256]{0:T(256)}, u32[]{:S(2)}) copy-start(s32[256]{0:T(256)} %param.10) | copy-start | bytes 3076
  7.2 11.0 %copy-start.11 = (bf16[256,1440]{0,1:T(8,128)(2,1)S(1)}, bf16[256,1440]{0,1:T(8,128)(2,1)}, u32[]{:S(2)}) copy-start(bf16[256,1440]{0,1:T(8,128)(2,1)} %param.8) | copy-start | bytes 2211844
  7.2 11.0 %copy-start.22 = (f32[256]{0:T(256)S(1)}, f32[256]{0:T(256)}, u32[]{:S(2)}) copy-start(f32[256]{0:T(256)} %param.9) | copy-start | bytes 3076
  7.2 118.6 %all-gather.3.cloned.1.call-start = ((), (), s32[]{:S(2)}) async-start(), calls=%async_computation.5 | async-start | bytes 5605376 | tf_op jit(solution)/shard_map/all_gather | solution.py:87
  10.5 9.8 %copy-start.2 = (bf16[80,2880]{1,0:T(8,128)(2,1)}, bf16[80,2880]{1,0:T(8,128)(2,1)S(1)}, u32[]{:S(2)}) copy-start(bf16[80,2880]{1,0:T(8,128)(2,1)S(1)} %fusion.114.refs_2_) | copy-start | bytes 1382404
  10.5 17.7 %collective-permute-start = (bf16[80,2880]{1,0:T(8,128)(2,1)S(1)}, bf16[80,2880]{1,0:T(8,128)(2,1)}, u32[]{:S(2)}, u32[]{:S(2)}) collective-permute-start(bf16[80,2880]{1,0:T(8,128)(2,1)S(1)} %fusion.114.refs_2_), channel_id=1, source_target_pairs={{0,32},{32,64},{64,96},{96,128},{128,160},{160,192},{192,224},{224... | collective-permute-start | bytes 1382408 | tf_op jit(solution)/shard_map/ppermute | solution.py:25
  15.3 14.5 %collective-permute-start.1 = (bf16[80,2880]{1,0:T(8,128)(2,1)S(1)}, bf16[80,2880]{1,0:T(8,128)(2,1)}, u32[]{:S(2)}, u32[]{:S(2)}) collective-permute-start(bf16[80,2880]{1,0:T(8,128)(2,1)S(1)} %fusion.114.refs_2_), channel_id=1, source_target_pairs={{0,480},{32,0},{64,32},{96,64},{128,96},{160,128},{192,160},{224,1... | collective-permute-start | bytes 1382408 | tf_op jit(solution)/shard_map/ppermute | solution.py:25
  18.2 2.1 copy-start.19
  18.2 2.2 copy-start.6
  20.3 1.5 copy-start.7
  29.8 24.3 %collective-permute-start.2 = (bf16[80,2880]{1,0:T(8,128)(2,1)}, bf16[80,2880]{1,0:T(8,128)(2,1)}, u32[]{:S(2)}, u32[]{:S(2)}) collective-permute-start(bf16[80,2880]{1,0:T(8,128)(2,1)} %collective-permute-done.refs_3_), channel_id=1, source_target_pairs={{0,32},{32,64},{64,96},{96,128},{128,160},{160,192},{192,224},{224... | collective-permute-start | bytes 1382408 | tf_op jit(solution)/shard_map/ppermute | solution.py:25
  32.7 25.2 %collective-permute-start.3 = (bf16[80,2880]{1,0:T(8,128)(2,1)}, bf16[80,2880]{1,0:T(8,128)(2,1)}, u32[]{:S(2)}, u32[]{:S(2)}) collective-permute-start(bf16[80,2880]{1,0:T(8,128)(2,1)} %collective-permute-done.1.refs_4_), channel_id=1, source_target_pairs={{0,480},{32,0},{64,32},{96,64},{128,96},{160,128},{192,160},{224,1... | collective-permute-start | bytes 1382408 | tf_op jit(solution)/shard_map/ppermute | solution.py:25
  35.1 31.7 %all-to-all-start = ((bf16[32,10,1440]{2,1,0:T(8,128)(2,1)}), bf16[32,10,1440]{2,1,0:T(8,128)(2,1)S(1)}, u32[]{:S(2)}, u32[]{:S(2)}) async-start(bf16[32,10,1440]{2,1,0:T(8,128)(2,1)} %reshape.130), calls=%async_computation | async-start | bytes 3145728 | tf_op jit(solution)/shard_map/all_to_all | solution.py:126
  44.6 165.5 %reduce-scatter.2.cloned.1.call-start = ((), (), s32[]{:S(2)}) async-start(), calls=%async_computation.4 | async-start | bytes 4804608 | tf_op jit(solution)/shard_map/reduce_scatter | solution.py:150
  44.7 2.7 %copy-start.9 = (bf16[320,1440]{1,0:T(8,128)(2,1)S(1)}, bf16[320,1440]{1,0:T(8,128)(2,1)}, u32[]{:S(2)}) copy-start(bf16[320,1440]{1,0:T(8,128)(2,1)} %fusion.74) | copy-start | bytes 2764804
  49.8 15.3 %copy-start.12 = (bf16[320,896]{1,0:T(8,128)(2,1)S(1)}, bf16[320,896]{1,0:T(8,128)(2,1)}, u32[]{:S(2)}) copy-start(bf16[320,896]{1,0:T(8,128)(2,1)} %fusion.103) | copy-start | bytes 1720324
  49.8 15.3 %copy-start.13 = (bf16[320,896]{1,0:T(8,128)(2,1)S(1)}, bf16[320,896]{1,0:T(8,128)(2,1)}, u32[]{:S(2)}) copy-start(bf16[320,896]{1,0:T(8,128)(2,1)} %fusion.94) | copy-start | bytes 1720324
  57.9 23.9 %collective-permute-start.4 = (bf16[80,2880]{1,0:T(8,128)(2,1)}, bf16[80,2880]{1,0:T(8,128)(2,1)}, u32[]{:S(2)}, u32[]{:S(2)}) collective-permute-start(bf16[80,2880]{1,0:T(8,128)(2,1)} %collective-permute-done.2.refs_5_), channel_id=1, source_target_pairs={{0,32},{32,64},{64,96},{96,128},{128,160},{160,192},{192,224},{224... | collective-permute-start | bytes 1382408 | tf_op jit(solution)/shard_map/ppermute | solution.py:25
  61.6 24.7 %collective-permute-start.5 = (bf16[80,2880]{1,0:T(8,128)(2,1)}, bf16[80,2880]{1,0:T(8,128)(2,1)}, u32[]{:S(2)}, u32[]{:S(2)}) collective-permute-start(bf16[80,2880]{1,0:T(8,128)(2,1)} %collective-permute-done.3.refs_6_), channel_id=1, source_target_pairs={{0,480},{32,0},{64,32},{96,64},{128,96},{160,128},{192,160},{224,1... | collective-permute-start | bytes 1382408 | tf_op jit(solution)/shard_map/ppermute | solution.py:25
  86.4 23.6 %collective-permute-start.6 = (bf16[80,2880]{1,0:T(8,128)(2,1)}, bf16[80,2880]{1,0:T(8,128)(2,1)S(1)}, u32[]{:S(2)}, u32[]{:S(2)}) collective-permute-start(bf16[80,2880]{1,0:T(8,128)(2,1)} %collective-permute-done.4.refs_7_), channel_id=1, source_target_pairs={{0,32},{32,64},{64,96},{96,128},{128,160},{160,192},{192,224},{224... | collective-permute-start | bytes 1382408 | tf_op jit(solution)/shard_map/ppermute | solution.py:25
  89.2 25.6 %collective-permute-start.7 = (bf16[80,2880]{1,0:T(8,128)(2,1)}, bf16[80,2880]{1,0:T(8,128)(2,1)}, u32[]{:S(2)}, u32[]{:S(2)}) collective-permute-start(bf16[80,2880]{1,0:T(8,128)(2,1)} %collective-permute-done.5.refs_8_), channel_id=1, source_target_pairs={{0,480},{32,0},{64,32},{96,64},{128,96},{160,128},{192,160},{224,1... | collective-permute-start | bytes 1382408 | tf_op jit(solution)/shard_map/ppermute | solution.py:25
  93.2 21.5 %copy-start.8 = (bf16[640,768]{1,0:T(8,128)(2,1)S(1)}, bf16[640,768]{1,0:T(8,128)(2,1)}, u32[]{:S(2)}) copy-start(bf16[640,768]{1,0:T(8,128)(2,1)} %pad_maximum_fusion.3) | copy-start | bytes 2949124
  95.4 19.4 %copy-start.1 = (bf16[640,2880]{1,0:T(8,128)(2,1)}, bf16[640,2880]{1,0:T(8,128)(2,1)S(1)}, u32[]{:S(2)}) copy-start(bf16[640,2880]{1,0:T(8,128)(2,1)S(1)} %fusion.27) | copy-start | bytes 11059204
  110.0 10.3 %copy-start.14 = (bf16[80,2880]{1,0:T(8,128)(2,1)}, bf16[80,2880]{1,0:T(8,128)(2,1)S(1)}, u32[]{:S(2)}) copy-start(bf16[80,2880]{1,0:T(8,128)(2,1)S(1)} %collective-permute-done.6.refs_9_) | copy-start | bytes 1382404
  120.3 10.3 %collective-permute-start.8 = (bf16[80,2880]{1,0:T(8,128)(2,1)S(1)}, bf16[80,2880]{1,0:T(8,128)(2,1)}, u32[]{:S(2)}, u32[]{:S(2)}) collective-permute-start(bf16[80,2880]{1,0:T(8,128)(2,1)S(1)} %collective-permute-done.6.refs_9_), channel_id=1, source_target_pairs={{0,32},{32,64},{64,96},{96,128},{128,160},{160,192},{192,224},{224... | collective-permute-start | bytes 1382408 | tf_op jit(solution)/shard_map/ppermute | solution.py:25
  123.7 11.3 %collective-permute-start.9 = (bf16[80,2880]{1,0:T(8,128)(2,1)}, bf16[80,2880]{1,0:T(8,128)(2,1)}, u32[]{:S(2)}, u32[]{:S(2)}) collective-permute-start(bf16[80,2880]{1,0:T(8,128)(2,1)} %collective-permute-done.7.refs_10_), channel_id=1, source_target_pairs={{0,480},{32,0},{64,32},{96,64},{128,96},{160,128},{192,160},{224,1... | collective-permute-start | bytes 1382408 | tf_op jit(solution)/shard_map/ppermute | solution.py:25
  129.0 20.3 %copy-start = (bf16[640,896]{1,0:T(8,128)(2,1)S(1)}, bf16[640,896]{1,0:T(8,128)(2,1)}, u32[]{:S(2)}) copy-start(bf16[640,896]{1,0:T(8,128)(2,1)} %get-tuple-element.45) | copy-start | bytes 3440644
  135.0 23.2 %collective-permute-start.10 = (bf16[80,2880]{1,0:T(8,128)(2,1)}, bf16[80,2880]{1,0:T(8,128)(2,1)S(1)}, u32[]{:S(2)}, u32[]{:S(2)}) collective-permute-start(bf16[80,2880]{1,0:T(8,128)(2,1)} %collective-permute-done.8.refs_11_), channel_id=1, source_target_pairs={{0,32},{32,64},{64,96},{96,128},{128,160},{160,192},{192,224},{224... | collective-permute-start | bytes 1382408 | tf_op jit(solution)/shard_map/ppermute | solution.py:25
  137.0 23.8 %collective-permute-start.11 = (bf16[80,2880]{1,0:T(8,128)(2,1)}, bf16[80,2880]{1,0:T(8,128)(2,1)S(1)}, u32[]{:S(2)}, u32[]{:S(2)}) collective-permute-start(bf16[80,2880]{1,0:T(8,128)(2,1)} %collective-permute-done.9.refs_12_), channel_id=1, source_target_pairs={{0,480},{32,0},{64,32},{96,64},{128,96},{160,128},{192,160},{224,1... | collective-permute-start | bytes 1382408 | tf_op jit(solution)/shard_map/ppermute | solution.py:25
  158.2 9.4 %copy-start.15 = (bf16[80,2880]{1,0:T(8,128)(2,1)}, bf16[80,2880]{1,0:T(8,128)(2,1)S(1)}, u32[]{:S(2)}) copy-start(bf16[80,2880]{1,0:T(8,128)(2,1)S(1)} %collective-permute-done.10.refs_13_) | copy-start | bytes 1382404
  160.7 6.9 %copy-start.16 = (bf16[80,2880]{1,0:T(8,128)(2,1)}, bf16[80,2880]{1,0:T(8,128)(2,1)S(1)}, u32[]{:S(2)}) copy-start(bf16[80,2880]{1,0:T(8,128)(2,1)S(1)} %collective-permute-done.11.refs_14_) | copy-start | bytes 1382404
  160.7 21.3 %collective-permute-start.12 = (bf16[80,2880]{1,0:T(8,128)(2,1)S(1)}, bf16[80,2880]{1,0:T(8,128)(2,1)S(1)}, u32[]{:S(2)}, u32[]{:S(2)}) collective-permute-start(bf16[80,2880]{1,0:T(8,128)(2,1)S(1)} %collective-permute-done.10.refs_13_), channel_id=1, source_target_pairs={{0,32},{32,64},{64,96},{96,128},{128,160},{160,192},{192,224},{224... | collective-permute-start | bytes 1382408 | tf_op jit(solution)/shard_map/ppermute | solution.py:25
  164.7 23.0 %collective-permute-start.13 = (bf16[80,2880]{1,0:T(8,128)(2,1)S(1)}, bf16[80,2880]{1,0:T(8,128)(2,1)S(1)}, u32[]{:S(2)}, u32[]{:S(2)}) collective-permute-start(bf16[80,2880]{1,0:T(8,128)(2,1)S(1)} %collective-permute-done.11.refs_14_), channel_id=1, source_target_pairs={{0,480},{32,0},{64,32},{96,64},{128,96},{160,128},{192,160},{224,1... | collective-permute-start | bytes 1382408 | tf_op jit(solution)/shard_map/ppermute | solution.py:25
  182.0 22.0 %copy-start.3 = (bf16[80,2880]{1,0:T(8,128)(2,1)}, bf16[80,2880]{1,0:T(8,128)(2,1)S(1)}, u32[]{:S(2)}) copy-start(bf16[80,2880]{1,0:T(8,128)(2,1)S(1)} %collective-permute-done.12.refs_1_) | copy-start | bytes 1382404
  187.7 19.1 %copy-start.10 = (bf16[80,2880]{1,0:T(8,128)(2,1)}, bf16[80,2880]{1,0:T(8,128)(2,1)S(1)}, u32[]{:S(2)}) copy-start(bf16[80,2880]{1,0:T(8,128)(2,1)S(1)} %collective-permute-done.13.refs_2_) | copy-start | bytes 1382404
  190.1 32.4 %all-to-all-start.1 = ((bf16[32,10,1200]{2,1,0:T(8,128)(2,1)}), bf16[32,10,1200]{2,1,0:T(8,128)(2,1)S(1)}, u32[]{:S(2)}, u32[]{:S(2)}) async-start(bf16[32,10,1200]{2,1,0:T(8,128)(2,1)} %reshape.134), calls=%async_computation.1 | async-start | bytes 2621440 | tf_op jit(solution)/shard_map/all_to_all | solution.py:169
  204.8 21.4 %collective-permute-start.14 = (bf16[48,2880]{1,0:T(8,128)(2,1)}, bf16[48,2880]{1,0:T(8,128)(2,1)}, u32[]{:S(2)}, u32[]{:S(2)}) collective-permute-start(bf16[48,2880]{1,0:T(8,128)(2,1)} %slice.59), channel_id=1, source_target_pairs={{0,32},{32,64},{64,96},{96,128},{128,160},{160,192},{192,224},{224... | collective-permute-start | bytes 829448 | tf_op jit(solution)/shard_map/ppermute | solution.py:25
  206.7 19.4 %collective-permute-start.15 = (bf16[32,2880]{1,0:T(8,128)(2,1)S(1)}, bf16[32,2880]{1,0:T(8,128)(2,1)S(1)}, u32[]{:S(2)}, u32[]{:S(2)}) collective-permute-start(bf16[32,2880]{1,0:T(8,128)(2,1)S(1)} %slice.60), channel_id=1, source_target_pairs={{0,480},{32,0},{64,32},{96,64},{128,96},{160,128},{192,160},{224,1... | collective-permute-start | bytes 552968 | tf_op jit(solution)/shard_map/ppermute | solution.py:25
  226.1 0.7 copy-start.17
  231.0 16.3 %copy-start.20 = (s32[256]{0:T(256)S(1)}, s32[256]{0:T(256)}, u32[]{:S(2)}) copy-start(s32[256]{0:T(256)} %copy-done.19) | copy-start | bytes 3076
  231.0 16.3 %copy-start.21 = (s32[240]{0:T(256)S(1)}, s32[240]{0:T(256)}, u32[]{:S(2)}) copy-start(s32[240]{0:T(256)} %pad_add_fusion) | copy-start | bytes 2884
  232.8 14.5 %all-to-all-start.2 = ((bf16[32,10,240]{2,1,0:T(8,128)(2,1)}), bf16[32,10,240]{2,1,0:T(8,128)(2,1)S(1)}, u32[]{:S(2)}, u32[]{:S(2)}) async-start(bf16[32,10,240]{2,1,0:T(8,128)(2,1)} %reshape.136), calls=%async_computation.2 | async-start | bytes 524288 | tf_op jit(solution)/shard_map/all_to_all | solution.py:169
Sparse Core Ops, SparseCore 0:
  10.4 107.3 all-gather.2
  120.6 88.8 reduce-scatter.1
